TPU v7x, 1024 devices: a whole 8x8x8 slice. The times are simulated.
1024 devices in a mesh: ep: 32 (over z, y_lo), rep: 32 (over y_hi, x, core).
Axes of the slice: x: 8, y: 8 (y_hi: 2, y_lo: 4; y = y_hi * 4 + y_lo), z: 8, core: 2. Of those that a mesh axis runs over, the one named last changes fastest.
Arguments:
- tokens: bfloat16 [1536, 4096], P('ep'), may hold values from -6 to 6
- cotangent: bfloat16 [1536, 4096], P('ep'), may hold values from -6 to 6
- routes: int32 [1536, 8], P('ep'), may hold values from 0 to 127, all different within a row; in each aligned block of 48 rows (0 to 47, 48 to 95, ...) at most 4 rows name the same one
- gate_probs: float32 [1536, 8], P('ep'), may hold values from 0.02 to 0.3
- gate_codes: bfloat16 [4096, 131072], P(None, ('ep', 'rep')), may hold values from -0.09375 to 0.09375
- gate_scales: float32 [32, 1024], P(None, ('ep', 'rep')), may hold values from 0.5 to 2
- up_codes: bfloat16 [4096, 131072], P(None, ('ep', 'rep')), may hold values from -0.09375 to 0.09375
- up_scales: float32 [32, 1024], P(None, ('ep', 'rep')), may hold values from 0.5 to 2
- down_codes: bfloat16 [131072, 4096], P(('ep', 'rep')), may hold values from -0.1875 to 0.1875
- down_scales: float32 [1024, 32], P(('ep', 'rep')), may hold values from 0.5 to 2
Outputs:
- mixed: bfloat16 [1536, 4096], P('ep', 'rep')
- d_tokens: bfloat16 [1536, 4096], P('ep', 'rep')
Inputs may be any that keep to these rules, and one draw needn't show every extreme that they name: `routes`: each row names 8 different experts. Among the 48 rows of one device (the aligned blocks of 48 rows), no expert is named more than 4 times, and in every draw some expert is named exactly 4 times within one block.
All inputs are finite; a program needn't handle non-finite values.
Results may differ from a plain program's by a relative error of at most 0.022.
Values may be sent and summed in bfloat16 or wider, within the bound.
A program may use at most 64 MiB of HBM per device.

v0:
```python
import jax
import jax.numpy as jnp
from jax import lax
from jax.sharding import PartitionSpec as P

EXP_EP = 4
TOP = 8
BLK = 128


def dequantize(quantized, scales):
    expanded = jnp.repeat(jnp.repeat(scales, BLK, axis=0), BLK, axis=1)
    return (quantized.astype(jnp.float32) * expanded).astype(jnp.bfloat16)


def silu_parts(gate_act):
    sigmoid = jax.nn.sigmoid(gate_act)
    return (gate_act * sigmoid, sigmoid * (1.0 + gate_act * (1.0 - sigmoid)))


def slot_selection(routes, gate_probs, dest_count, capacity):
    experts_all = EXP_EP * dest_count
    flattened = routes.reshape(-1)
    onehot = (flattened[:, None] == jnp.arange(experts_all, dtype=jnp.int32)[None, :]).astype(
        jnp.int32
    )
    before = jnp.cumsum(onehot, axis=0) - onehot
    slot_rank = jnp.sum(before * onehot, axis=1).reshape(routes.shape)
    wanted = (
        jnp.arange(EXP_EP, dtype=jnp.int32)[:, None]
        + EXP_EP * jnp.arange(dest_count, dtype=jnp.int32)[None, :]
    )
    slot_iota = jnp.arange(capacity, dtype=jnp.int32)
    matches = (routes[None, None, None, :, :] == wanted[:, :, None, None, None]) & (
        slot_rank[None, None, None, :, :] == slot_iota[None, None, :, None, None]
    )
    chosen = jnp.any(matches, axis=4)
    weighted = jnp.sum(jnp.where(matches, gate_probs[None, None, None, :, :], 0.0), axis=4)
    return (chosen, weighted)


def per_device(
    tokens,
    cotangent,
    routes,
    gate_probs,
    gate_codes,
    gate_scales,
    up_codes,
    up_scales,
    down_codes,
    down_scales,
):
    dest_count = lax.axis_size("ep")
    columns = lax.axis_size("rep")
    shards = columns // EXP_EP
    my_block = lax.axis_index("rep") // shards
    tok_rows, model_width = tokens.shape
    capacity = max(2, 4 * tok_rows * TOP // (3 * EXP_EP * dest_count))
    chosen, weighted = slot_selection(routes, gate_probs, dest_count, capacity)
    slots_all = dest_count * capacity
    chosen_mine = (
        lax.dynamic_index_in_dim(chosen, my_block, 0, keepdims=False)
        .reshape(slots_all, tok_rows)
        .astype(jnp.bfloat16)
    )
    weighted_mine = lax.dynamic_index_in_dim(weighted, my_block, 0, keepdims=False).reshape(
        slots_all, tok_rows
    )
    send_rows = (
        jnp.dot(chosen_mine, tokens, preferred_element_type=jnp.float32)
        .astype(jnp.bfloat16)
        .reshape(dest_count, capacity, model_width)
    )
    send_grads = (
        jnp.dot(weighted_mine, cotangent.astype(jnp.float32), precision=lax.Precision.HIGHEST)
        .astype(jnp.bfloat16)
        .reshape(dest_count, capacity, model_width)
    )
    w_gate = dequantize(gate_codes, gate_scales)
    w_up = dequantize(up_codes, up_scales)
    w_down = dequantize(down_codes, down_scales)
    slot_rows = lax.all_to_all(send_rows, "ep", split_axis=0, concat_axis=0, tiled=True)
    slot_grads = lax.all_to_all(send_grads, "ep", split_axis=0, concat_axis=0, tiled=True)
    slot_count = slot_rows.shape[1]
    flat_rows = slot_rows.reshape(-1, model_width)
    flat_grads = slot_grads.reshape(-1, model_width)
    gate_act = jnp.dot(flat_rows, w_gate, preferred_element_type=jnp.float32)
    up_act = jnp.dot(flat_rows, w_up, preferred_element_type=jnp.float32)
    activation, derivative = silu_parts(gate_act)
    hidden = (activation * up_act).astype(jnp.bfloat16)
    out_term = jnp.dot(hidden, w_down, preferred_element_type=jnp.float32).astype(jnp.bfloat16)
    hidden_grad = lax.dot_general(
        flat_grads, w_down, (((1,), (1,)), ((), ())), preferred_element_type=jnp.float32
    )
    gate_grad = (hidden_grad * up_act * derivative).astype(jnp.bfloat16)
    up_grad = (hidden_grad * activation).astype(jnp.bfloat16)
    dx_term = (
        lax.dot_general(
            gate_grad, w_gate, (((1,), (1,)), ((), ())), preferred_element_type=jnp.float32
        )
        + lax.dot_general(
            up_grad, w_up, (((1,), (1,)), ((), ())), preferred_element_type=jnp.float32
        )
    ).astype(jnp.bfloat16)
    out_term, dx_term = (
        out_term.reshape(dest_count, slot_count, model_width),
        dx_term.reshape(dest_count, slot_count, model_width),
    )
    back_out, back_dx = (
        lax.all_to_all(out_term, "ep", split_axis=0, concat_axis=0, tiled=True),
        lax.all_to_all(dx_term, "ep", split_axis=0, concat_axis=0, tiled=True),
    )
    token_out = lax.dot_general(
        chosen_mine,
        back_out.reshape(slots_all, model_width),
        (((0,), (0,)), ((), ())),
        preferred_element_type=jnp.float32,
    )
    token_dx = lax.dot_general(
        chosen_mine,
        back_dx.reshape(slots_all, model_width),
        (((0,), (0,)), ((), ())),
        preferred_element_type=jnp.float32,
    )
    mixed, d_tokens = (
        lax.psum_scatter(
            token_out.astype(jnp.bfloat16), "rep", scatter_dimension=1, tiled=True
        ).astype(jnp.float32),
        lax.psum_scatter(
            token_dx.astype(jnp.bfloat16), "rep", scatter_dimension=1, tiled=True
        ).astype(jnp.float32),
    )
    return (mixed.astype(jnp.bfloat16), d_tokens.astype(jnp.bfloat16))


def solution(mesh):
    placed = (
        P("ep", None),
        P("ep", None),
        P("ep", None),
        P("ep", None),
        P(None, ("ep", "rep")),
        P(None, ("ep", "rep")),
        P(None, ("ep", "rep")),
        P(None, ("ep", "rep")),
        P(("ep", "rep"), None),
        P(("ep", "rep"), None),
    )
    return jax.shard_map(
        per_device,
        mesh=mesh,
        in_specs=placed,
        out_specs=(P("ep", "rep"), P("ep", "rep")),
        check_vma=False,
    )
```

profile of v0, /device:TPU:14, one launch (start us, length us, event | category | flops | bytes accessed | tf_op | source)
XLA Modules:
  0.0 422.3 jit_solution(14084927134007456649)
XLA Ops:
  7.2 0.0 copy-start
  7.2 0.8 copy.26
  8.0 0.1 eq.70
  8.1 0.1 eq.66
  8.2 0.1 copy.28
  8.3 0.9 broadcast_compare_fusion
  9.2 0.2 fusion.6
  9.5 0.1 broadcast_add_fusion
  9.6 0.2 fusion.9
  9.8 0.1 eq.74
  9.9 0.1 copy.30
  10.0 0.7 and_reduce_fusion
  10.7 0.0 copy-done
  10.8 0.4 convolution_convert_fusion.2
  11.2 0.0 copy-start.14
  11.2 0.0 copy-start.7
  11.2 1.2 reshape.115
  12.4 20.5 %all-to-all-start = ((bf16[32,4,4096]{2,1,0:T(4,128)(2,1)}), bf16[32,4,4096]{2,1,0:T(4,128)(2,1)S(1)}, u32[]{:S(2)}, u32[]{:S(2)}) async-start(bf16[32,4,4096]{2,1,0:T(4,128)(2,1)} %reshape.115), calls=%async_computation | async-start | bytes 2097152 | tf_op jit(solution)/shard_map/all_to_all | solution.py:83
  32.9 0.0 copy-done.14
  32.9 0.9 fusion.1
  33.8 0.0 copy-done.7
  33.8 1.0 convolution_convert_fusion
  34.7 1.2 reshape.122
  36.0 24.3 %all-to-all-done = bf16[32,4,4096]{2,1,0:T(4,128)(2,1)S(1)} async-done(((bf16[32,4,4096]{2,1,0:T(4,128)(2,1)}), bf16[32,4,4096]{2,1,0:T(4,128)(2,1)S(1)}, u32[]{:S(2)}, u32[]{:S(2)}) %all-to-all-start) | async-done | bytes 1048608 | tf_op jit(solution)/shard_map/all_to_all | solution.py:83
  60.3 6.5 %all-to-all-start.2 = ((bf16[32,4,4096]{2,1,0:T(4,128)(2,1)}), bf16[32,4,4096]{2,1,0:T(4,128)(2,1)S(1)}, u32[]{:S(2)}, u32[]{:S(2)}) async-start(bf16[32,4,4096]{2,1,0:T(4,128)(2,1)} %reshape.122), calls=%async_computation.2 | async-start | bytes 2097152 | tf_op jit(solution)/shard_map/all_to_all | solution.py:84
  66.8 1.3 broadcast_bitcast_fusion.2
  68.1 1.3 broadcast_bitcast_fusion.1
  69.4 1.3 broadcast_bitcast_fusion
  70.8 1.1 reshape.116
  71.8 0.0 copy-done.1
  71.9 0.0 copy-start.13
  71.9 2.2 fusion.4
  74.1 2.0 fusion.5
  76.1 0.0 copy-done.5
  76.1 0.0 copy-start.8
  76.2 0.6 copy-done.8
  76.8 0.4 convolution_convert_fusion.1
  77.2 1.2 reshape.119
  78.4 15.2 %all-to-all-done.2 = bf16[32,4,4096]{2,1,0:T(4,128)(2,1)S(1)} async-done(((bf16[32,4,4096]{2,1,0:T(4,128)(2,1)}), bf16[32,4,4096]{2,1,0:T(4,128)(2,1)S(1)}, u32[]{:S(2)}, u32[]{:S(2)}) %all-to-all-start.2) | async-done | bytes 1048608 | tf_op jit(solution)/shard_map/all_to_all | solution.py:84
  93.6 6.7 %all-to-all-start.1 = ((bf16[32,4,4096]{2,1,0:T(4,128)(2,1)}), bf16[32,4,4096]{2,1,0:T(4,128)(2,1)S(1)}, u32[]{:S(2)}, u32[]{:S(2)}) async-start(bf16[32,4,4096]{2,1,0:T(4,128)(2,1)} %reshape.119), calls=%async_computation.1 | async-start | bytes 2097152 | tf_op jit(solution)/shard_map/all_to_all | solution.py:111
  100.3 1.2 reshape.123
  101.5 2.0 fusion.2
  103.6 0.0 copy-start.4
  103.6 0.8 fusion.3
  104.5 0.3 copy-done.4
  104.8 1.1 fusion
  105.9 1.2 reshape.124
  107.2 19.8 %all-to-all-done.1 = bf16[32,4,4096]{2,1,0:T(4,128)(2,1)S(1)} async-done(((bf16[32,4,4096]{2,1,0:T(4,128)(2,1)}), bf16[32,4,4096]{2,1,0:T(4,128)(2,1)S(1)}, u32[]{:S(2)}, u32[]{:S(2)}) %all-to-all-start.1) | async-done | bytes 1048608 | tf_op jit(solution)/shard_map/all_to_all | solution.py:111
  127.0 6.4 %all-to-all-start.3 = ((bf16[32,4,4096]{2,1,0:T(4,128)(2,1)}), bf16[32,4,4096]{2,1,0:T(4,128)(2,1)S(1)}, u32[]{:S(2)}, u32[]{:S(2)}) async-start(bf16[32,4,4096]{2,1,0:T(4,128)(2,1)} %reshape.124), calls=%async_computation.3 | async-start | bytes 2097152 | tf_op jit(solution)/shard_map/all_to_all | solution.py:112
  133.4 0.0 reduce-scatter.7.cloned.1.call-start
  133.5 0.3 reshape.120
  133.7 0.3 convolution_convert_fusion.4
  134.1 1.3 copy.31
  135.4 0.0 reduce-scatter.7.cloned.1.call-update
  135.4 0.0 reduce-scatter.9.cloned.1.call-start
  135.5 24.5 %all-to-all-done.3 = bf16[32,4,4096]{2,1,0:T(4,128)(2,1)S(1)} async-done(((bf16[32,4,4096]{2,1,0:T(4,128)(2,1)}), bf16[32,4,4096]{2,1,0:T(4,128)(2,1)S(1)}, u32[]{:S(2)}, u32[]{:S(2)}) %all-to-all-start.3) | async-done | bytes 1048608 | tf_op jit(solution)/shard_map/all_to_all | solution.py:112
  160.0 0.3 reshape.125
  160.3 0.3 convolution_convert_fusion.3
  160.6 1.4 copy.33
  162.0 0.0 reduce-scatter.9.cloned.1.call-update
  162.0 113.1 %reduce-scatter.7.cloned.1.call-done = bf16[128,48]{1,0:T(8,128)(2,1)} async-done(((bf16[4096,48]{1,0:T(8,128)(2,1)}), bf16[128,48]{1,0:T(8,128)(2,1)}) %reduce-scatter.7.cloned.1.call-update) | async-done | bytes 12304
  275.0 1.4 copy.32
  276.5 137.6 %reduce-scatter.9.cloned.1.call-done = bf16[128,48]{1,0:T(8,128)(2,1)} async-done(((bf16[4096,48]{1,0:T(8,128)(2,1)}), bf16[128,48]{1,0:T(8,128)(2,1)}) %reduce-scatter.9.cloned.1.call-update) | async-done | bytes 12304
  414.0 1.4 copy.34
  (25 shorter events, 0.1 us)
Async XLA Ops:
  7.2 3.6 copy-start
  11.2 21.7 %copy-start.14 = (f32[48,8]{0,1:T(8,128)S(1)}, f32[48,8]{0,1:T(8,128)}, u32[]{:S(2)}) copy-start(f32[48,8]{0,1:T(8,128)} %param.13) | copy-start | bytes 4612
  11.2 22.6 %copy-start.7 = (bf16[48,4096]{1,0:T(8,128)(2,1)S(1)}, bf16[48,4096]{1,0:T(8,128)(2,1)}, u32[]{:S(2)}) copy-start(bf16[48,4096]{1,0:T(8,128)(2,1)} %param.11) | copy-start | bytes 1179652
  12.4 47.9 %all-to-all-start = ((bf16[32,4,4096]{2,1,0:T(4,128)(2,1)}), bf16[32,4,4096]{2,1,0:T(4,128)(2,1)S(1)}, u32[]{:S(2)}, u32[]{:S(2)}) async-start(bf16[32,4,4096]{2,1,0:T(4,128)(2,1)} %reshape.115), calls=%async_computation | async-start | bytes 2097152 | tf_op jit(solution)/shard_map/all_to_all | solution.py:83
  36.0 35.9 %copy-start.1 = (bf16[4096,128]{1,0:T(8,128)(2,1)S(1)}, bf16[4096,128]{1,0:T(8,128)(2,1)}, u32[]{:S(2)}) copy-start(bf16[4096,128]{1,0:T(8,128)(2,1)} %param.14) | copy-start | bytes 3145732
  60.3 33.3 %all-to-all-start.2 = ((bf16[32,4,4096]{2,1,0:T(4,128)(2,1)}), bf16[32,4,4096]{2,1,0:T(4,128)(2,1)S(1)}, u32[]{:S(2)}, u32[]{:S(2)}) async-start(bf16[32,4,4096]{2,1,0:T(4,128)(2,1)} %reshape.122), calls=%async_computation.2 | async-start | bytes 2097152 | tf_op jit(solution)/shard_map/all_to_all | solution.py:84
  71.9 2.2 copy-start.3
  71.9 2.2 copy-start.10
  71.9 4.9 %copy-start.2 = (bf16[128,4096]{1,0:T(8,128)(2,1)S(1)}, bf16[128,4096]{1,0:T(8,128)(2,1)}, u32[]{:S(2)}) copy-start(bf16[128,4096]{1,0:T(8,128)(2,1)} %param.18) | copy-start | bytes 3145732
  71.9 4.9 %copy-start.13 = (f32[4096]{0:T(1024)S(1)}, f32[4096]{0:T(1024)}, u32[]{:S(2)}) copy-start(f32[4096]{0:T(1024)} %broadcast_bitcast_fusion) | copy-start | bytes 49156
  74.1 2.1 copy-start.5
  76.1 0.6 copy-start.8
  93.6 33.3 %all-to-all-start.1 = ((bf16[32,4,4096]{2,1,0:T(4,128)(2,1)}), bf16[32,4,4096]{2,1,0:T(4,128)(2,1)S(1)}, u32[]{:S(2)}, u32[]{:S(2)}) async-start(bf16[32,4,4096]{2,1,0:T(4,128)(2,1)} %reshape.119), calls=%async_computation.1 | async-start | bytes 2097152 | tf_op jit(solution)/shard_map/all_to_all | solution.py:111
  101.5 2.0 copy-start.6
  101.5 2.0 copy-start.9
  101.5 2.1 copy-start.12
  103.6 1.2 copy-start.4
  103.6 1.2 copy-start.11
  127.0 33.0 %all-to-all-start.3 = ((bf16[32,4,4096]{2,1,0:T(4,128)(2,1)}), bf16[32,4,4096]{2,1,0:T(4,128)(2,1)S(1)}, u32[]{:S(2)}, u32[]{:S(2)}) async-start(bf16[32,4,4096]{2,1,0:T(4,128)(2,1)} %reshape.124), calls=%async_computation.3 | async-start | bytes 2097152 | tf_op jit(solution)/shard_map/all_to_all | solution.py:112
  133.4 141.6 %reduce-scatter.7.cloned.1.call-start = ((), (), s32[]{:S(2)}) async-start(), calls=%async_computation.6 | async-start | bytes 1081344
  135.4 278.6 %reduce-scatter.9.cloned.1.call-start = ((), (), s32[]{:S(2)}) async-start(), calls=%async_computation.7 | async-start | bytes 1081344
Sparse Core Ops, SparseCore 0:
  140.0 134.9 reduce-scatter.6
  280.8 133.1 reduce-scatter.8
where the time goes:
time: 424 us; the launch traced here: 422 us
  waiting for transfers between devices  334 us (79%)
  starting transfers between devices  40.2 us (9%)
  local copies, waits for them, and re-layouts  19.6 us (5%)
  between operations  14.4 us (3%)
  matrix products  10.7 us (3%)
    unnamed x4, waiting for transfers between devices  251 us
    all_to_all x1, waiting for transfers between devices, per_device(): lax.all_to_all(dx_term, 'ep', split_axis=0, concat_axis=0, tiled=True)  24.5 us
    all_to_all x1, waiting for transfers between devices, per_device(): lax.all_to_all(send_rows, 'ep', split_axis=0, concat_axis=0, tiled=True)  24.3 us
    all_to_all x1, starting transfers between devices, per_device(): lax.all_to_all(send_rows, 'ep', split_axis=0, concat_axis=0, tiled=True)  20.5 us
    all_to_all x1, waiting for transfers between devices, per_device(): lax.all_to_all(out_term, 'ep', split_axis=0, concat_axis=0, tiled=True)  19.8 us
    all_to_all x1, waiting for transfers between devices, per_device(): lax.all_to_all(send_grads, 'ep', split_axis=0, concat_axis=0, tiled=True)  15.2 us
  transfers between devices with their start and end apart: 6, of which 6 were waited for; matrix products, arithmetic and copies ran while one was open for 6% of the time, Pallas kernels for 0%

commit v1 on v0

v1 whole, which is shorter than its diff:
```python
import jax
import jax.numpy as jnp
from jax import lax
from jax.experimental import pallas as pl
from jax.experimental.pallas import tpu as pltpu
from jax.sharding import PartitionSpec as P

EXP_EP = 4
TOP = 8
BLK = 128
CAP = 4
ROWS = 16
MESH = pl.DeviceIdType.MESH
NT = (((1,), (1,)), ((), ()))
F32 = jnp.float32
BF16 = jnp.bfloat16


def dot(a, b):
    return jnp.dot(a, b, preferred_element_type=F32)


def kernel(
    n,
    tok,
    cot,
    routes,
    probs,
    gate_s,
    up_s,
    down_s,
    gate_c,
    up_c,
    down_c,
    mixed,
    d_tok,
    raw_g,
    raw_u,
    raw_d,
    w_gu,
    w_d,
    sel,
    send,
    x_all,
    acc_gu,
    acc_d,
    hid,
    grad,
    term,
    from_sib,
    from_nbr,
    pair,
    back,
    fin,
    fin_in,
    load_sem,
    eps,
    epr,
    share_s,
    share_r,
    red_s,
    red_r,
    eps2,
    epr2,
    fin_s,
    fin_r,
):
    s = lax.axis_index("ep")
    r = lax.axis_index("rep")
    core = lax.rem(r, 2)
    xp = lax.rem(r // 2, 2)
    g = lax.rem(r, 4)
    u = r // 4
    block = r // 8
    sib = (s, r + 1 - 2 * core)
    nbr = (s, r + 2 - 4 * xp)
    tok_rows, width = tok.shape
    half = width // 2
    quarter = width // 4
    lanes = 2 * BLK

    def peer(k):
        return lax.rem(s + k, n)

    loads = [
        pltpu.make_async_copy(src, dst, load_sem.at[i])
        for i, (src, dst) in enumerate(((gate_c, raw_g), (up_c, raw_u), (down_c, raw_d)))
    ]
    for load in loads:
        load.start()

    barrier = pltpu.get_barrier_semaphore()

    def greet(k, carry):
        pl.semaphore_signal(barrier, inc=1, device_id=(peer(k), r), device_id_type=MESH)
        return carry

    def greet_final(v, carry):
        pl.semaphore_signal(
            barrier, inc=1, device_id=(s, lax.rem(u + v, 8) * 4 + g), device_id_type=MESH
        )
        return carry

    lax.fori_loop(1, n, greet, 0)
    lax.fori_loop(1, 8, greet_final, 0)
    pl.semaphore_signal(barrier, inc=1, device_id=sib, device_id_type=MESH)
    pl.semaphore_signal(barrier, inc=1, device_id=nbr, device_id_type=MESH)

    rows8 = n * 8
    ri = lax.broadcasted_iota(jnp.int32, (rows8, tok_rows), 0)
    away = s + ri // 8
    away = jnp.where(away >= n, away - n, away)
    wanted = (EXP_EP * away + block).astype(F32)
    eye = (
        lax.broadcasted_iota(jnp.int32, (TOP, TOP), 0)
        == lax.broadcasted_iota(jnp.int32, (TOP, TOP), 1)
    ).astype(F32)
    routes_f = routes[...].astype(F32)
    routes_t = lax.dot_general(
        eye, routes_f, NT, precision=lax.Precision.HIGHEST, preferred_element_type=F32
    )
    probs_t = lax.dot_general(
        eye, probs[...], NT, precision=lax.Precision.HIGHEST, preferred_element_type=F32
    )
    named = jnp.zeros((rows8, tok_rows), F32)
    weight = jnp.zeros((rows8, tok_rows), F32)
    for k in range(TOP):
        hit = jnp.abs(routes_t[k : k + 1, :] - wanted) < 0.5
        named = jnp.where(hit, 1.0, named)
        weight = jnp.where(hit, probs_t[k : k + 1, :], weight)
    ti = lax.broadcasted_iota(jnp.int32, (tok_rows, tok_rows), 0)
    tj = lax.broadcasted_iota(jnp.int32, (tok_rows, tok_rows), 1)
    rank = dot(named.astype(BF16), (ti < tj).astype(F32).astype(BF16))
    slot = lax.rem(ri, CAP).astype(F32)
    chosen = jnp.where(rank == slot, named, 0.0)
    array_of = lax.rem(ri // CAP, 2)
    row_weight = jnp.sum(chosen * jnp.where(array_of == 0, 1.0, weight), axis=1, keepdims=True)
    pick_tok = jnp.where(array_of == 0, chosen, 0.0).astype(BF16)
    pick_cot = jnp.where(array_of == 1, chosen, 0.0).astype(BF16)

    def piece(ref, start):
        lo = pl.multiple_of(start, BLK)
        hi = pl.multiple_of(start + quarter, BLK)
        return jnp.concatenate([ref[:, pl.ds(lo, BLK)], ref[:, pl.ds(hi, BLK)]], axis=1)

    for h in range(2):
        parts = []
        for q in range(2):
            start = q * half + (4 * h + g) * BLK
            rows = dot(pick_tok, piece(tok, start)) + dot(pick_cot, piece(cot, start))
            parts.append((rows * row_weight).reshape(n, 8, lanes))
        send[h] = jnp.concatenate(parts, axis=1).astype(BF16)
        x_all[4 * h + g, 0] = send[h, 0]

    pl.semaphore_wait(barrier, n - 1 + 7 + 2)

    for h in range(2):

        def go(k, carry, h=h):
            pltpu.make_async_remote_copy(
                src_ref=send.at[h, k],
                dst_ref=x_all.at[4 * h + g, k],
                send_sem=eps.at[h],
                recv_sem=epr.at[h],
                device_id=(peer(k), r),
                device_id_type=MESH,
            ).start()
            return carry

        lax.fori_loop(1, n, go, 0)

    rows16 = n * ROWS
    li = lax.broadcasted_iota(jnp.int32, (tok_rows, rows16), 1)
    away = s + li // ROWS
    away = jnp.where(away >= n, away - n, away)
    wanted = EXP_EP * away + block
    named = jnp.zeros((tok_rows, rows16), F32)
    for k in range(TOP):
        named = jnp.where(routes[:, k : k + 1] == wanted, 1.0, named)
    rank = dot((tj < ti).astype(F32).astype(BF16), named.astype(BF16))
    chosen = jnp.where(rank == lax.rem(li, CAP).astype(F32), named, 0.0)
    kind = lax.rem(li // CAP, 4)
    for i in range(4):
        sel[i * tok_rows : (i + 1) * tok_rows, :] = jnp.where(kind == i, chosen, 0.0).astype(BF16)

    for load in loads:
        load.wait()

    def expand(ch, carry):
        j = lax.rem(ch, 8)
        at = pl.ds(pl.multiple_of((ch // 8) * BLK, BLK), BLK)
        src = pl.ds(pl.multiple_of(ch * BLK, BLK), BLK)
        w_gu[j, at, 0:BLK] = (raw_g[src, :].astype(F32) * gate_s[ch, 0]).astype(BF16)
        w_gu[j, at, BLK : 2 * BLK] = (raw_u[src, :].astype(F32) * up_s[ch, 0]).astype(BF16)
        w_d[j, :, at] = (raw_d[:, src].astype(F32) * down_s[0, ch]).astype(BF16)
        return carry

    lax.fori_loop(0, width // BLK, expand, 0)

    acc_gu[...] = jnp.zeros_like(acc_gu)
    acc_d[...] = jnp.zeros_like(acc_d)

    def first(j):
        got = x_all[j].astype(F32)
        flat = jnp.concatenate(
            [got[:, 0:8].reshape(rows8, lanes), got[:, 8:16].reshape(rows8, lanes)], axis=1
        ).astype(BF16)
        acc_gu[...] += dot(flat, w_gu[j])
        acc_d[...] += lax.dot_general(flat, w_d[j], NT, preferred_element_type=F32)

    def bulk_wait(ref, sem):
        pltpu.make_async_copy(ref, ref, sem).wait()

    def share(h, way):
        j = 4 * h + (g if way < 2 else g + 2 - 4 * xp)
        return pltpu.make_async_remote_copy(
            src_ref=x_all.at[j],
            dst_ref=x_all.at[j],
            send_sem=share_s.at[h, way],
            recv_sem=share_r.at[h, way],
            device_id=nbr if way == 1 else sib,
            device_id_type=MESH,
        )

    def arrived(h, way):
        j = 4 * h + (
            (g + 1 - 2 * core, g + 2 - 4 * xp, g + 1 - 2 * core + 2 - 4 * xp)[way]
        )
        bulk_wait(x_all.at[j], share_r.at[h, way])
        return j

    def own(h):
        bulk_wait(x_all.at[4 * h + g, pl.ds(1, n - 1)], epr.at[h])
        for way in (1, 0):
            share(h, way).start()
        return 4 * h + g

    j = own(0)
    first(j)
    j = arrived(0, 0)
    first(j)
    j1 = own(1)
    j = arrived(0, 1)
    share(0, 2).start()
    first(j1)
    first(j)
    j = arrived(1, 0)
    first(j)
    j = arrived(0, 2)
    first(j)
    j = arrived(1, 1)
    share(1, 2).start()
    first(j)
    j = arrived(1, 2)
    first(j)

    gate = acc_gu[:, 0:BLK].reshape(n, 8, BLK)
    up = acc_gu[:, BLK : 2 * BLK].reshape(n, 8, BLK)
    hid_grad = acc_d[...].reshape(n, 8, BLK)
    grad_row = lax.broadcasted_iota(jnp.int32, (n, 8, BLK), 1) >= CAP
    sigmoid = jax.nn.sigmoid(gate)
    act = gate * sigmoid
    slope = sigmoid * (1.0 + gate * (1.0 - sigmoid))

    def swap(v):
        return jnp.concatenate([v[:, CAP:], v[:, :CAP]], axis=1)

    hid[...] = jnp.where(grad_row, 0.0, act * up).reshape(rows8, BLK).astype(BF16)
    gate_grad = jnp.where(grad_row, hid_grad * swap(up * slope), 0.0)
    up_grad = jnp.where(grad_row, hid_grad * swap(act), 0.0)
    grad[:, 0:BLK] = gate_grad.reshape(rows8, BLK).astype(BF16)
    grad[:, BLK : 2 * BLK] = up_grad.reshape(rows8, BLK).astype(BF16)

    def second(j):
        rows = dot(hid[...], w_d[j]) + lax.dot_general(
            grad[...], w_gu[j], NT, preferred_element_type=F32
        )
        return jnp.concatenate(
            [rows[:, :lanes].reshape(n, 8, lanes), rows[:, lanes:].reshape(n, 8, lanes)], axis=1
        )

    def to_sib(h, kept):
        xq = xp if kept else 1 - xp
        i = 2 * h + kept
        term[i] = second(4 * h + 2 * xq + 1 - core).astype(BF16)
        copy = pltpu.make_async_remote_copy(
            src_ref=term.at[i],
            dst_ref=from_sib.at[i],
            send_sem=red_s.at[i],
            recv_sem=red_r.at[i],
            device_id=sib,
            device_id_type=MESH,
        )
        copy.start()
        return copy

    sib_copies = {}
    nbr_copies = {}
    for h in range(2):
        sib_copies[h, 0] = to_sib(h, 0)
    for h in range(2):
        value = second(4 * h + 2 * (1 - xp) + core)
        sib_copies[h, 0].wait_recv()
        pair[2 + h] = (value + from_sib[2 * h].astype(F32)).astype(BF16)
        nbr_copies[h] = pltpu.make_async_remote_copy(
            src_ref=pair.at[2 + h],
            dst_ref=from_nbr.at[h],
            send_sem=red_s.at[4 + h],
            recv_sem=red_r.at[4 + h],
            device_id=nbr,
            device_id_type=MESH,
        )
        nbr_copies[h].start()
    for h in range(2):
        sib_copies[h, 1] = to_sib(h, 1)
    for h in range(2):
        value = second(4 * h + 2 * xp + core)
        sib_copies[h, 1].wait_recv()
        value = value + from_sib[2 * h + 1].astype(F32)
        nbr_copies[h].wait_recv()
        pair[h] = (value + from_nbr[h].astype(F32)).astype(BF16)

        def go_back(k, carry, h=h):
            pltpu.make_async_remote_copy(
                src_ref=pair.at[h, k],
                dst_ref=back.at[h, k],
                send_sem=eps2.at[h],
                recv_sem=epr2.at[h],
                device_id=(lax.rem(s + n - k, n), r),
                device_id_type=MESH,
            ).start()
            return carry

        lax.fori_loop(1, n, go_back, 0)
        back[h, 0] = pair[h, 0]

    for h in range(2):
        bulk_wait(back.at[h, pl.ds(1, n - 1)], epr2.at[h])
        sums = dot(sel[...], back[h].reshape(rows16, lanes))
        for q in range(2):
            for b in range(2):
                fin[4 * q + 2 * b + h] = sums[
                    q * 2 * tok_rows : (q + 1) * 2 * tok_rows, b * BLK : (b + 1) * BLK
                ].astype(BF16)

    def go_final(v, carry):
        to = lax.rem(u + v, 8)
        pltpu.make_async_remote_copy(
            src_ref=fin.at[to],
            dst_ref=fin_in.at[v],
            send_sem=fin_s.at[v],
            recv_sem=fin_r,
            device_id=(s, to * 4 + g),
            device_id_type=MESH,
        ).start()
        return carry

    lax.fori_loop(1, 8, go_final, 0)
    bulk_wait(fin_in.at[pl.ds(1, 7)], fin_r)
    total = fin[u].astype(F32)
    for v in range(1, 8):
        total = total + fin_in[v].astype(F32)
    mixed[...] = total[:tok_rows].astype(BF16)
    d_tok[...] = total[tok_rows:].astype(BF16)

    def sent(v, carry):
        bulk_wait(fin.at[v], fin_s.at[v])
        return carry

    lax.fori_loop(1, 8, sent, 0)
    for h in range(2):
        bulk_wait(send.at[h, pl.ds(1, n - 1)], eps.at[h])
        bulk_wait(pair.at[h, pl.ds(1, n - 1)], eps2.at[h])
        for way in range(3):
            share(h, way).wait_send()
        nbr_copies[h].wait_send()
        for kept in range(2):
            sib_copies[h, kept].wait_send()


def per_device(
    tokens,
    cotangent,
    routes,
    gate_probs,
    gate_codes,
    gate_scales,
    up_codes,
    up_scales,
    down_codes,
    down_scales,
):
    n = lax.axis_size("ep")
    tok_rows, width = tokens.shape
    lanes = 2 * BLK
    vmem = pl.BlockSpec(memory_space=pltpu.VMEM)
    smem = pl.BlockSpec(memory_space=pltpu.SMEM)
    hbm = pl.BlockSpec(memory_space=pl.ANY)
    out = jax.ShapeDtypeStruct((tok_rows, BLK), BF16)
    dma = pltpu.SemaphoreType.DMA

    def body(*refs):
        kernel(n, *refs)

    return pl.pallas_call(
        body,
        out_shape=(out, out),
        in_specs=[vmem] * 4 + [smem] * 3 + [hbm] * 3,
        out_specs=(vmem, vmem),
        scratch_shapes=[
            pltpu.VMEM((width, BLK), BF16),
            pltpu.VMEM((width, BLK), BF16),
            pltpu.VMEM((BLK, width), BF16),
            pltpu.VMEM((8, 4 * BLK, 2 * BLK), BF16),
            pltpu.VMEM((8, BLK, 4 * BLK), BF16),
            pltpu.VMEM((4 * tok_rows, n * ROWS), BF16),
            pltpu.VMEM((2, n, ROWS, lanes), BF16),
            pltpu.VMEM((8, n, ROWS, lanes), BF16),
            pltpu.VMEM((n * 8, 2 * BLK), F32),
            pltpu.VMEM((n * 8, BLK), F32),
            pltpu.VMEM((n * 8, BLK), BF16),
            pltpu.VMEM((n * 8, 2 * BLK), BF16),
            pltpu.VMEM((4, n, ROWS, lanes), BF16),
            pltpu.VMEM((4, n, ROWS, lanes), BF16),
            pltpu.VMEM((2, n, ROWS, lanes), BF16),
            pltpu.VMEM((4, n, ROWS, lanes), BF16),
            pltpu.VMEM((2, n, ROWS, lanes), BF16),
            pltpu.VMEM((8, 2 * tok_rows, BLK), BF16),
            pltpu.VMEM((8, 2 * tok_rows, BLK), BF16),
            dma((3,)),
            dma((2,)),
            dma((2,)),
            dma((2, 3)),
            dma((2, 3)),
            dma((6,)),
            dma((6,)),
            dma((2,)),
            dma((2,)),
            dma((8,)),
            dma,
        ],
        compiler_params=pltpu.CompilerParams(
            collective_id=0, has_side_effects=True, vmem_limit_bytes=40 * 1024 * 1024
        ),
        cost_estimate=pl.CostEstimate(
            flops=2 * 9 * n * 8 * width * BLK,
            bytes_accessed=2 * 3 * width * BLK,
            transcendentals=n * 8 * BLK,
        ),
    )(
        tokens,
        cotangent,
        routes,
        gate_probs,
        gate_scales,
        up_scales,
        down_scales,
        gate_codes,
        up_codes,
        down_codes,
    )


def solution(mesh):
    placed = (
        P("ep", None),
        P("ep", None),
        P("ep", None),
        P("ep", None),
        P(None, ("ep", "rep")),
        P(None, ("ep", "rep")),
        P(None, ("ep", "rep")),
        P(None, ("ep", "rep")),
        P(("ep", "rep"), None),
        P(("ep", "rep"), None),
    )
    return jax.shard_map(
        per_device,
        mesh=mesh,
        in_specs=placed,
        out_specs=(P("ep", "rep"), P("ep", "rep")),
        check_vma=False,
    )
```

time: 424 us -> 93.8 us (0.22)
  waiting for transfers between devices: 334 us -> 0 us
  Pallas kernels: 0 us -> 83.1 us
  starting transfers between devices: 40.2 us -> 0 us
  between operations: 14.4 us -> 0.66 us
  matrix products: 10.7 us -> 0 us
  local copies, waits for them, and re-layouts: 19.6 us -> 9.64 us
    unnamed x4 -> x0, waiting for transfers between devices: 251 us -> none
    all_to_all x4 -> x0, waiting for transfers between devices: 83.8 us -> none  [the longest x1 24.5 us: per_device(): lax.all_to_all(dx_term, 'ep', split_axis=0, concat_axis=0, tiled=True)]
    pallas_call x0 -> x1, Pallas kernels: none -> 83.1 us  [per_device(): pl.pallas_call(body, out_shape=(out, out), in_specs=[vmem] * 4 + [smem] *...]
    all_to_all x4 -> x0, starting transfers between devices: 40.1 us -> none  [the longest x1 20.5 us: per_device(): lax.all_to_all(send_rows, 'ep', split_axis=0, concat_axis=0, tiled=True)]
    dot_general x10 -> x0, matrix products: 10.7 us -> none  [the longest x1 2.17 us: per_device(): gate_act = jnp.dot(flat_rows, w_gate, preferred_element_type=jnp.float32)]
    reshape x8 -> x0, local copies, waits for them, and re-layouts: 7.72 us -> none  [the longest x1 1.24 us: per_device(): send_grads = jnp.dot(weighted_mine, cotangent.astype(jnp.float32), precis...]
    unnamed x35 -> x24, local copies, waits for them, and re-layouts: 7.4 us -> 9.64 us
  transfers between devices with their start and end apart: 6 -> 0, of which waited for: 6 -> 0; matrix products, arithmetic and copies ran while one was open for 6% -> 0% of each run, Pallas kernels for 0% -> 0%
where the time goes in v1:
time: 93.8 us; the launch traced here: 93.3 us
  Pallas kernels  83.1 us (89%)
  local copies, waits for them, and re-layouts  9.64 us (10%)
    pallas_call x1, Pallas kernels, per_device(): pl.pallas_call(body, out_shape=(out, out), in_specs=[vmem] * 4 + [smem] *...  83.1 us
    unnamed x24, local copies, waits for them, and re-layouts  9.64 us

profile of v1, /device:TPU:14, one launch (start us, length us, event | category | flops | bytes accessed | tf_op | source)
XLA Modules:
  0.0 93.3 jit_solution(7337378054587789420)
XLA Ops:
  0.6 0.0 copy-start.8
  0.6 0.7 copy.14.refs_4_
  1.4 0.0 copy-done.8
  1.4 0.0 copy-start.6
  1.4 0.1 copy.15.refs_5_
  1.5 0.6 copy-done.6
  2.1 0.0 copy-start.7
  2.1 0.1 copy.12.refs_2_
  2.2 0.6 copy-done.7
  2.8 0.0 copy-start.5
  2.8 0.1 copy.13.refs_3_
  2.8 0.6 copy-done.5
  3.4 0.0 copy-start
  3.4 1.2 %copy-done = bf16[4096,128]{1,0:T(8,128)(2,1)S(1)} copy-done((bf16[4096,128]{1,0:T(8,128)(2,1)S(1)}, bf16[4096,128]{1,0:T(8,128)(2,1)}, u32[]{:S(2)}) %copy-start) | copy-done | bytes 1048600
  4.6 0.0 copy-start.1
  4.6 1.2 %copy-done.1 = bf16[4096,128]{1,0:T(8,128)(2,1)S(1)} copy-done((bf16[4096,128]{1,0:T(8,128)(2,1)S(1)}, bf16[4096,128]{1,0:T(8,128)(2,1)}, u32[]{:S(2)}) %copy-start.1) | copy-done | bytes 1048600
  5.9 0.0 copy-start.2
  5.9 1.2 %copy-done.2 = bf16[128,4096]{1,0:T(8,128)(2,1)S(1)} copy-done((bf16[128,4096]{1,0:T(8,128)(2,1)S(1)}, bf16[128,4096]{1,0:T(8,128)(2,1)}, u32[]{:S(2)}) %copy-start.2) | copy-done | bytes 1048600
  7.1 0.0 copy-start.3
  7.1 1.0 %copy-done.3 = bf16[48,4096]{1,0:T(8,128)(2,1)S(1)} copy-done((bf16[48,4096]{1,0:T(8,128)(2,1)S(1)}, bf16[48,4096]{1,0:T(8,128)(2,1)}, u32[]{:S(2)}) %copy-start.3) | copy-done | bytes 393240
  8.1 0.0 copy-start.4
  8.1 1.0 %copy-done.4 = bf16[48,4096]{1,0:T(8,128)(2,1)S(1)} copy-done((bf16[48,4096]{1,0:T(8,128)(2,1)S(1)}, bf16[48,4096]{1,0:T(8,128)(2,1)}, u32[]{:S(2)}) %copy-start.4) | copy-done | bytes 393240
  9.1 83.1 %shard_map.113 = (bf16[48,128]{1,0:T(8,128)(2,1)S(1)}, bf16[48,128]{1,0:T(8,128)(2,1)S(1)}) custom-call(bf16[48,4096]{1,0:T(8,128)(2,1)S(1)} %copy-done.3, bf16[48,4096]{1,0:T(8,128)(2,1)S(1)} %copy-done.4, s32[48,8]{1,0:T(8,128)S(1)} %copy.12.refs_2_, f32[48,8]{1,0:T(8,128)S(1)} %copy.13.refs_3_, f32[32,1]{1,0:T(8,128)S(1)} %copy.14.refs_4_, ...), custom_call_target="tpu_custom_call" | custom-call | flops 2415919104 | bytes 3145728 | tf_op jit(solution)/shard_map/pallas_call | solution.py:405
  92.1 0.6 copy.18
  92.7 0.6 copy.19
Async XLA Ops:
  0.6 0.8 copy-start.8
  1.4 0.7 copy-start.6
  2.1 0.7 copy-start.7
  2.8 0.7 copy-start.5
  3.4 1.2 %copy-start = (bf16[4096,128]{1,0:T(8,128)(2,1)S(1)}, bf16[4096,128]{1,0:T(8,128)(2,1)}, u32[]{:S(2)}) copy-start(bf16[4096,128]{1,0:T(8,128)(2,1)} %refs_7_.1) | copy-start | bytes 3145732
  4.6 1.2 %copy-start.1 = (bf16[4096,128]{1,0:T(8,128)(2,1)S(1)}, bf16[4096,128]{1,0:T(8,128)(2,1)}, u32[]{:S(2)}) copy-start(bf16[4096,128]{1,0:T(8,128)(2,1)} %refs_8_.1) | copy-start | bytes 3145732
  5.9 1.2 %copy-start.2 = (bf16[128,4096]{1,0:T(8,128)(2,1)S(1)}, bf16[128,4096]{1,0:T(8,128)(2,1)}, u32[]{:S(2)}) copy-start(bf16[128,4096]{1,0:T(8,128)(2,1)} %refs_9_.1) | copy-start | bytes 3145732
  7.1 1.0 %copy-start.3 = (bf16[48,4096]{1,0:T(8,128)(2,1)S(1)}, bf16[48,4096]{1,0:T(8,128)(2,1)}, u32[]{:S(2)}) copy-start(bf16[48,4096]{1,0:T(8,128)(2,1)} %refs_0_.1) | copy-start | bytes 1179652
  8.1 1.0 %copy-start.4 = (bf16[48,4096]{1,0:T(8,128)(2,1)S(1)}, bf16[48,4096]{1,0:T(8,128)(2,1)}, u32[]{:S(2)}) copy-start(bf16[48,4096]{1,0:T(8,128)(2,1)} %refs_1_.1) | copy-start | bytes 1179652

commit v2 on v1

--- a/solution.py
+++ b/solution.py
@@ -22,6 +22,18 @@
 
 def kernel(
     n,
+    tok_h,
+    cot_h,
+    routes_h,
+    probs_h,
+    gate_sh,
+    up_sh,
+    down_sh,
+    gate_c,
+    up_c,
+    down_c,
+    mixed,
+    d_tok,
     tok,
     cot,
     routes,
@@ -29,11 +41,6 @@
     gate_s,
     up_s,
     down_s,
-    gate_c,
-    up_c,
-    down_c,
-    mixed,
-    d_tok,
     raw_g,
     raw_u,
     raw_d,
@@ -50,6 +57,7 @@
     from_sib,
     from_nbr,
     pair,
+    mine,
     back,
     fin,
     fin_in,
@@ -79,12 +87,31 @@
     quarter = width // 4
     lanes = 2 * BLK
 
-    def peer(k):
+    def away_of(i):
+        k = jnp.where(lax.rem(i, 2) == 1, (i + 1) // 2, n - i // 2)
         return lax.rem(s + k, n)
 
+    def back_of(i):
+        k = jnp.where(lax.rem(i, 2) == 1, (i + 1) // 2, n - i // 2)
+        return lax.rem(s + n - k, n)
+
+    def part(p):
+        return pl.ds(p * (n // 2), n // 2)
+
+    pairs = (
+        (routes_h, routes),
+        (probs_h, probs),
+        (tok_h, tok),
+        (cot_h, cot),
+        (gate_sh, gate_s),
+        (up_sh, up_s),
+        (down_sh, down_s),
+        (gate_c, raw_g),
+        (up_c, raw_u),
+        (down_c, raw_d),
+    )
     loads = [
-        pltpu.make_async_copy(src, dst, load_sem.at[i])
-        for i, (src, dst) in enumerate(((gate_c, raw_g), (up_c, raw_u), (down_c, raw_d)))
+        pltpu.make_async_copy(src, dst, load_sem.at[i]) for i, (src, dst) in enumerate(pairs)
     ]
     for load in loads:
         load.start()
@@ -92,7 +119,7 @@
     barrier = pltpu.get_barrier_semaphore()
 
     def greet(k, carry):
-        pl.semaphore_signal(barrier, inc=1, device_id=(peer(k), r), device_id_type=MESH)
+        pl.semaphore_signal(barrier, inc=1, device_id=(away_of(k), r), device_id_type=MESH)
         return carry
 
     def greet_final(v, carry):
@@ -106,10 +133,12 @@
     pl.semaphore_signal(barrier, inc=1, device_id=sib, device_id_type=MESH)
     pl.semaphore_signal(barrier, inc=1, device_id=nbr, device_id_type=MESH)
 
+    for load in loads[:4]:
+        load.wait()
+
     rows8 = n * 8
     ri = lax.broadcasted_iota(jnp.int32, (rows8, tok_rows), 0)
-    away = s + ri // 8
-    away = jnp.where(away >= n, away - n, away)
+    away = away_of(ri // 8)
     wanted = (EXP_EP * away + block).astype(F32)
     eye = (
         lax.broadcasted_iota(jnp.int32, (TOP, TOP), 0)
@@ -117,17 +146,18 @@
     ).astype(F32)
     routes_f = routes[...].astype(F32)
     routes_t = lax.dot_general(
-        eye, routes_f, NT, precision=lax.Precision.HIGHEST, preferred_element_type=F32
-    )
-    probs_t = lax.dot_general(
-        eye, probs[...], NT, precision=lax.Precision.HIGHEST, preferred_element_type=F32
+        routes_f,
+        eye,
+        (((0,), (0,)), ((), ())),
+        precision=lax.Precision.HIGHEST,
+        preferred_element_type=F32,
     )
     named = jnp.zeros((rows8, tok_rows), F32)
     weight = jnp.zeros((rows8, tok_rows), F32)
     for k in range(TOP):
-        hit = jnp.abs(routes_t[k : k + 1, :] - wanted) < 0.5
+        hit = jnp.abs(routes_f[k : k + 1, :] - wanted) < 0.5
         named = jnp.where(hit, 1.0, named)
-        weight = jnp.where(hit, probs_t[k : k + 1, :], weight)
+        weight = jnp.where(hit, probs[k : k + 1, :], weight)
     ti = lax.broadcasted_iota(jnp.int32, (tok_rows, tok_rows), 0)
     tj = lax.broadcasted_iota(jnp.int32, (tok_rows, tok_rows), 1)
     rank = dot(named.astype(BF16), (ti < tj).astype(F32).astype(BF16))
@@ -151,47 +181,45 @@
             parts.append((rows * row_weight).reshape(n, 8, lanes))
         send[h] = jnp.concatenate(parts, axis=1).astype(BF16)
         x_all[4 * h + g, 0] = send[h, 0]
-
-    pl.semaphore_wait(barrier, n - 1 + 7 + 2)
-
-    for h in range(2):
-
-        def go(k, carry, h=h):
-            pltpu.make_async_remote_copy(
-                src_ref=send.at[h, k],
-                dst_ref=x_all.at[4 * h + g, k],
-                send_sem=eps.at[h],
-                recv_sem=epr.at[h],
-                device_id=(peer(k), r),
-                device_id_type=MESH,
-            ).start()
-            return carry
-
-        lax.fori_loop(1, n, go, 0)
+        if h == 0:
+            pl.semaphore_wait(barrier, n - 1 + 7 + 2)
+        for p in range(2):
+
+            def go(i, carry, h=h, p=p):
+                pltpu.make_async_remote_copy(
+                    src_ref=send.at[h, i],
+                    dst_ref=x_all.at[4 * h + g, i],
+                    send_sem=eps.at[h],
+                    recv_sem=epr.at[h, p],
+                    device_id=(away_of(i), r),
+                    device_id_type=MESH,
+                ).start()
+                return carry
+
+            lax.fori_loop(max(1, p * (n // 2)), (p + 1) * (n // 2), go, 0)
 
     rows16 = n * ROWS
     li = lax.broadcasted_iota(jnp.int32, (tok_rows, rows16), 1)
-    away = s + li // ROWS
-    away = jnp.where(away >= n, away - n, away)
-    wanted = EXP_EP * away + block
+    away = away_of(li // ROWS)
+    wanted = (EXP_EP * away + block).astype(F32)
     named = jnp.zeros((tok_rows, rows16), F32)
     for k in range(TOP):
-        named = jnp.where(routes[:, k : k + 1] == wanted, 1.0, named)
+        named = jnp.where(jnp.abs(routes_t[:, k : k + 1] - wanted) < 0.5, 1.0, named)
     rank = dot((tj < ti).astype(F32).astype(BF16), named.astype(BF16))
     chosen = jnp.where(rank == lax.rem(li, CAP).astype(F32), named, 0.0)
     kind = lax.rem(li // CAP, 4)
     for i in range(4):
         sel[i * tok_rows : (i + 1) * tok_rows, :] = jnp.where(kind == i, chosen, 0.0).astype(BF16)
 
-    for load in loads:
+    for load in loads[4:]:
         load.wait()
 
     def expand(ch, carry):
         j = lax.rem(ch, 8)
         at = pl.ds(pl.multiple_of((ch // 8) * BLK, BLK), BLK)
         src = pl.ds(pl.multiple_of(ch * BLK, BLK), BLK)
-        w_gu[j, at, 0:BLK] = (raw_g[src, :].astype(F32) * gate_s[ch, 0]).astype(BF16)
-        w_gu[j, at, BLK : 2 * BLK] = (raw_u[src, :].astype(F32) * up_s[ch, 0]).astype(BF16)
+        w_gu[j, at, 0:BLK] = (raw_g[src, :].astype(F32) * gate_s[0, ch]).astype(BF16)
+        w_gu[j, at, BLK : 2 * BLK] = (raw_u[src, :].astype(F32) * up_s[0, ch]).astype(BF16)
         w_d[j, :, at] = (raw_d[:, src].astype(F32) * down_s[0, ch]).astype(BF16)
         return carry
 
@@ -211,48 +239,58 @@
     def bulk_wait(ref, sem):
         pltpu.make_async_copy(ref, ref, sem).wait()
 
-    def share(h, way):
+    def landed(p):
+        return pl.ds(1, n // 2 - 1) if p == 0 else part(1)
+
+    def share(h, p, way):
         j = 4 * h + (g if way < 2 else g + 2 - 4 * xp)
         return pltpu.make_async_remote_copy(
-            src_ref=x_all.at[j],
-            dst_ref=x_all.at[j],
-            send_sem=share_s.at[h, way],
-            recv_sem=share_r.at[h, way],
+            src_ref=x_all.at[j, part(p)],
+            dst_ref=x_all.at[j, part(p)],
+            send_sem=share_s.at[h, p, way],
+            recv_sem=share_r.at[h, p, way],
             device_id=nbr if way == 1 else sib,
             device_id_type=MESH,
         )
 
-    def arrived(h, way):
-        j = 4 * h + (
+    def source(h, way):
+        return 4 * h + (
             (g + 1 - 2 * core, g + 2 - 4 * xp, g + 1 - 2 * core + 2 - 4 * xp)[way]
         )
-        bulk_wait(x_all.at[j], share_r.at[h, way])
-        return j
-
-    def own(h):
-        bulk_wait(x_all.at[4 * h + g, pl.ds(1, n - 1)], epr.at[h])
-        for way in (1, 0):
-            share(h, way).start()
-        return 4 * h + g
-
-    j = own(0)
-    first(j)
-    j = arrived(0, 0)
-    first(j)
-    j1 = own(1)
-    j = arrived(0, 1)
-    share(0, 2).start()
-    first(j1)
-    first(j)
-    j = arrived(1, 0)
-    first(j)
-    j = arrived(0, 2)
-    first(j)
-    j = arrived(1, 1)
-    share(1, 2).start()
-    first(j)
-    j = arrived(1, 2)
-    first(j)
+
+    def arrived(h, p, way):
+        bulk_wait(x_all.at[source(h, way), part(p)], share_r.at[h, p, way])
+
+    def own(h, p):
+        bulk_wait(x_all.at[4 * h + g, landed(p)], epr.at[h, p])
+        share(h, p, 1).start()
+        share(h, p, 0).start()
+
+    def forward(h, p):
+        arrived(h, p, 1)
+        share(h, p, 2).start()
+
+    def take(h, way):
+        for p in range(2):
+            arrived(h, p, way)
+        first(source(h, way))
+
+    own(0, 0)
+    own(0, 1)
+    first(g)
+    forward(0, 0)
+    take(0, 0)
+    own(1, 0)
+    forward(0, 1)
+    first(source(0, 1))
+    own(1, 1)
+    first(4 + g)
+    forward(1, 0)
+    take(0, 2)
+    take(1, 0)
+    forward(1, 1)
+    first(source(1, 1))
+    take(1, 2)
 
     gate = acc_gu[:, 0:BLK].reshape(n, 8, BLK)
     up = acc_gu[:, BLK : 2 * BLK].reshape(n, 8, BLK)
@@ -302,60 +340,76 @@
         value = second(4 * h + 2 * (1 - xp) + core)
         sib_copies[h, 0].wait_recv()
         pair[2 + h] = (value + from_sib[2 * h].astype(F32)).astype(BF16)
-        nbr_copies[h] = pltpu.make_async_remote_copy(
-            src_ref=pair.at[2 + h],
-            dst_ref=from_nbr.at[h],
-            send_sem=red_s.at[4 + h],
-            recv_sem=red_r.at[4 + h],
-            device_id=nbr,
-            device_id_type=MESH,
-        )
-        nbr_copies[h].start()
+        for p in range(2):
+            nbr_copies[h, p] = pltpu.make_async_remote_copy(
+                src_ref=pair.at[2 + h, part(p)],
+                dst_ref=from_nbr.at[h, part(p)],
+                send_sem=red_s.at[4 + 2 * h + p],
+                recv_sem=red_r.at[4 + 2 * h + p],
+                device_id=nbr,
+                device_id_type=MESH,
+            )
+            nbr_copies[h, p].start()
     for h in range(2):
         sib_copies[h, 1] = to_sib(h, 1)
     for h in range(2):
         value = second(4 * h + 2 * xp + core)
         sib_copies[h, 1].wait_recv()
-        value = value + from_sib[2 * h + 1].astype(F32)
-        nbr_copies[h].wait_recv()
-        pair[h] = (value + from_nbr[h].astype(F32)).astype(BF16)
-
-        def go_back(k, carry, h=h):
-            pltpu.make_async_remote_copy(
-                src_ref=pair.at[h, k],
-                dst_ref=back.at[h, k],
-                send_sem=eps2.at[h],
-                recv_sem=epr2.at[h],
-                device_id=(lax.rem(s + n - k, n), r),
-                device_id_type=MESH,
-            ).start()
-            return carry
-
-        lax.fori_loop(1, n, go_back, 0)
+        mine[h] = value + from_sib[2 * h + 1].astype(F32)
+    for h in range(2):
+        for p in range(2):
+            nbr_copies[h, p].wait_recv()
+            pair[h, part(p)] = (
+                mine[h, part(p)] + from_nbr[h, part(p)].astype(F32)
+            ).astype(BF16)
+
+            def go_back(i, carry, h=h, p=p):
+                pltpu.make_async_remote_copy(
+                    src_ref=pair.at[h, i],
+                    dst_ref=back.at[h, i],
+                    send_sem=eps2.at[h],
+                    recv_sem=epr2.at[h, p],
+                    device_id=(back_of(i), r),
+                    device_id_type=MESH,
+                ).start()
+                return carry
+
+            lax.fori_loop(max(1, p * (n // 2)), (p + 1) * (n // 2), go_back, 0)
         back[h, 0] = pair[h, 0]
 
-    for h in range(2):
-        bulk_wait(back.at[h, pl.ds(1, n - 1)], epr2.at[h])
-        sums = dot(sel[...], back[h].reshape(rows16, lanes))
+    half_rows = rows16 // 2
+    for h in range(2):
+        sums = None
+        for p in range(2):
+            bulk_wait(back.at[h, landed(p)], epr2.at[h, p])
+            more = dot(
+                sel[:, p * half_rows : (p + 1) * half_rows],
+                back[h, part(p)].reshape(half_rows, lanes),
+            )
+            sums = more if p == 0 else sums + more
         for q in range(2):
             for b in range(2):
                 fin[4 * q + 2 * b + h] = sums[
                     q * 2 * tok_rows : (q + 1) * 2 * tok_rows, b * BLK : (b + 1) * BLK
                 ].astype(BF16)
 
-    def go_final(v, carry):
-        to = lax.rem(u + v, 8)
-        pltpu.make_async_remote_copy(
-            src_ref=fin.at[to],
-            dst_ref=fin_in.at[v],
-            send_sem=fin_s.at[v],
-            recv_sem=fin_r,
-            device_id=(s, to * 4 + g),
-            device_id_type=MESH,
-        ).start()
-        return carry
-
-    lax.fori_loop(1, 8, go_final, 0)
+        def go_final(w, carry, h=h):
+            to = 2 * w + h
+
+            @pl.when(to != u)
+            def _():
+                pltpu.make_async_remote_copy(
+                    src_ref=fin.at[to],
+                    dst_ref=fin_in.at[lax.rem(to + 8 - u, 8)],
+                    send_sem=fin_s,
+                    recv_sem=fin_r,
+                    device_id=(s, to * 4 + g),
+                    device_id_type=MESH,
+                ).start()
+
+            return carry
+
+        lax.fori_loop(0, 4, go_final, 0)
     bulk_wait(fin_in.at[pl.ds(1, 7)], fin_r)
     total = fin[u].astype(F32)
     for v in range(1, 8):
@@ -363,17 +417,14 @@
     mixed[...] = total[:tok_rows].astype(BF16)
     d_tok[...] = total[tok_rows:].astype(BF16)
 
-    def sent(v, carry):
-        bulk_wait(fin.at[v], fin_s.at[v])
-        return carry
-
-    lax.fori_loop(1, 8, sent, 0)
+    bulk_wait(fin_in.at[pl.ds(1, 7)], fin_s)
     for h in range(2):
         bulk_wait(send.at[h, pl.ds(1, n - 1)], eps.at[h])
         bulk_wait(pair.at[h, pl.ds(1, n - 1)], eps2.at[h])
-        for way in range(3):
-            share(h, way).wait_send()
-        nbr_copies[h].wait_send()
+        for p in range(2):
+            for way in range(3):
+                share(h, p, way).wait_send()
+            nbr_copies[h, p].wait_send()
         for kept in range(2):
             sib_copies[h, kept].wait_send()
 
@@ -394,7 +445,6 @@
     tok_rows, width = tokens.shape
     lanes = 2 * BLK
     vmem = pl.BlockSpec(memory_space=pltpu.VMEM)
-    smem = pl.BlockSpec(memory_space=pltpu.SMEM)
     hbm = pl.BlockSpec(memory_space=pl.ANY)
     out = jax.ShapeDtypeStruct((tok_rows, BLK), BF16)
     dma = pltpu.SemaphoreType.DMA
@@ -405,9 +455,16 @@
     return pl.pallas_call(
         body,
         out_shape=(out, out),
-        in_specs=[vmem] * 4 + [smem] * 3 + [hbm] * 3,
+        in_specs=[hbm] * 10,
         out_specs=(vmem, vmem),
         scratch_shapes=[
+            pltpu.VMEM((tok_rows, width), BF16),
+            pltpu.VMEM((tok_rows, width), BF16),
+            pltpu.VMEM((TOP, tok_rows), jnp.int32),
+            pltpu.VMEM((TOP, tok_rows), F32),
+            pltpu.SMEM((1, width // BLK), F32),
+            pltpu.SMEM((1, width // BLK), F32),
+            pltpu.SMEM((1, width // BLK), F32),
             pltpu.VMEM((width, BLK), BF16),
             pltpu.VMEM((width, BLK), BF16),
             pltpu.VMEM((BLK, width), BF16),
@@ -424,23 +481,24 @@
             pltpu.VMEM((4, n, ROWS, lanes), BF16),
             pltpu.VMEM((2, n, ROWS, lanes), BF16),
             pltpu.VMEM((4, n, ROWS, lanes), BF16),
+            pltpu.VMEM((2, n, ROWS, lanes), F32),
             pltpu.VMEM((2, n, ROWS, lanes), BF16),
             pltpu.VMEM((8, 2 * tok_rows, BLK), BF16),
             pltpu.VMEM((8, 2 * tok_rows, BLK), BF16),
-            dma((3,)),
+            dma((10,)),
             dma((2,)),
+            dma((2, 2)),
+            dma((2, 2, 3)),
+            dma((2, 2, 3)),
+            dma((8,)),
+            dma((8,)),
             dma((2,)),
-            dma((2, 3)),
-            dma((2, 3)),
-            dma((6,)),
-            dma((6,)),
-            dma((2,)),
-            dma((2,)),
-            dma((8,)),
+            dma((2, 2)),
+            dma,
             dma,
         ],
         compiler_params=pltpu.CompilerParams(
-            collective_id=0, has_side_effects=True, vmem_limit_bytes=40 * 1024 * 1024
+            collective_id=0, has_side_effects=True, vmem_limit_bytes=60 * 1024 * 1024
         ),
         cost_estimate=pl.CostEstimate(
             flops=2 * 9 * n * 8 * width * BLK,
@@ -450,10 +508,10 @@
     )(
         tokens,
         cotangent,
-        routes,
-        gate_probs,
-        gate_scales,
-        up_scales,
+        routes.T,
+        gate_probs.T,
+        gate_scales.T,
+        up_scales.T,
         down_scales,
         gate_codes,
         up_codes,

time: 93.8 us -> 82 us (0.87)
  local copies, waits for them, and re-layouts: 9.64 us -> 1.92 us
  Pallas kernels: 83.1 us -> 78.7 us
    unnamed x24 -> x4, local copies, waits for them, and re-layouts: 9.64 us -> 1.92 us
    pallas_call x1, Pallas kernels: 83.1 us -> 78.7 us  [per_device(): pl.pallas_call(body, out_shape=(out, out), in_specs=[hbm] * 10, out_specs...]
where the time goes in v2:
time: 82 us; the launch traced here: 81.3 us
  Pallas kernels  78.7 us (96%)
  local copies, waits for them, and re-layouts  1.92 us (2%)
    pallas_call x1, Pallas kernels, per_device(): pl.pallas_call(body, out_shape=(out, out), in_specs=[hbm] * 10, out_specs...  78.7 us
    unnamed x4, local copies, waits for them, and re-layouts  1.92 us

profile of v2, /device:TPU:14, one launch (start us, length us, event | category | flops | bytes accessed | tf_op | source)
XLA Modules:
  0.0 81.3 jit_solution(1955336078591166234)
XLA Ops:
  0.6 78.7 %shard_map.113 = (bf16[48,128]{1,0:T(8,128)(2,1)}, bf16[48,128]{1,0:T(8,128)(2,1)}) custom-call(bf16[48,4096]{1,0:T(8,128)(2,1)} %refs_0_.1, bf16[48,4096]{1,0:T(8,128)(2,1)} %refs_1_.1, s32[8,48]{1,0:T(8,128)} %bitcast.4, f32[8,48]{1,0:T(8,128)} %bitcast.5, f32[1,32]{1,0:T(1,128)} %bitcast.6, f32[1,32]{1,0:T(1,128)} %bitcast.7, f32[1,32]{1,0:T(1,128)} %refs_6_.1, ...), custom_call_target="tpu_custom_call" | custom-call | flops 2415919104 | bytes 3145728 | tf_op jit(solution)/shard_map/pallas_call | solution.py:455
  79.3 0.0 copy-start
  79.4 1.3 %copy.14 = bf16[48,128]{1,0:T(8,128)(2,1)} copy(bf16[48,128]{1,0:T(8,128)(2,1)} %get-tuple-element.4) | data formatting | bytes 24576
  80.7 0.0 copy-done
  80.7 0.6 copy.15
Async XLA Ops:
  79.3 1.3 %copy-start = (bf16[48,128]{1,0:T(8,128)(2,1)S(1)}, bf16[48,128]{1,0:T(8,128)(2,1)}, u32[]{:S(2)}) copy-start(bf16[48,128]{1,0:T(8,128)(2,1)} %get-tuple-element.5) | copy-start | bytes 36868

commit v3 on v2

--- a/solution.py
+++ b/solution.py
@@ -9,6 +9,7 @@
 TOP = 8
 BLK = 128
 CAP = 4
+PARTS = 4
 ROWS = 16
 MESH = pl.DeviceIdType.MESH
 NT = (((1,), (1,)), ((), ()))
@@ -32,8 +33,7 @@
     gate_c,
     up_c,
     down_c,
-    mixed,
-    d_tok,
+    sums_out,
     tok,
     cot,
     routes,
@@ -96,7 +96,7 @@
         return lax.rem(s + n - k, n)
 
     def part(p):
-        return pl.ds(p * (n // 2), n // 2)
+        return pl.ds(p * (n // PARTS), n // PARTS)
 
     pairs = (
         (routes_h, routes),
@@ -133,7 +133,7 @@
     pl.semaphore_signal(barrier, inc=1, device_id=sib, device_id_type=MESH)
     pl.semaphore_signal(barrier, inc=1, device_id=nbr, device_id_type=MESH)
 
-    for load in loads[:4]:
+    for load in loads[:2]:
         load.wait()
 
     rows8 = n * 8
@@ -173,6 +173,9 @@
         hi = pl.multiple_of(start + quarter, BLK)
         return jnp.concatenate([ref[:, pl.ds(lo, BLK)], ref[:, pl.ds(hi, BLK)]], axis=1)
 
+    for load in loads[2:4]:
+        load.wait()
+
     for h in range(2):
         parts = []
         for q in range(2):
@@ -183,7 +186,7 @@
         x_all[4 * h + g, 0] = send[h, 0]
         if h == 0:
             pl.semaphore_wait(barrier, n - 1 + 7 + 2)
-        for p in range(2):
+        for p in range(PARTS):
 
             def go(i, carry, h=h, p=p):
                 pltpu.make_async_remote_copy(
@@ -196,7 +199,7 @@
                 ).start()
                 return carry
 
-            lax.fori_loop(max(1, p * (n // 2)), (p + 1) * (n // 2), go, 0)
+            lax.fori_loop(max(1, p * (n // PARTS)), (p + 1) * (n // PARTS), go, 0)
 
     rows16 = n * ROWS
     li = lax.broadcasted_iota(jnp.int32, (tok_rows, rows16), 1)
@@ -240,7 +243,7 @@
         pltpu.make_async_copy(ref, ref, sem).wait()
 
     def landed(p):
-        return pl.ds(1, n // 2 - 1) if p == 0 else part(1)
+        return pl.ds(1, n // PARTS - 1) if p == 0 else part(p)
 
     def share(h, p, way):
         j = 4 * h + (g if way < 2 else g + 2 - 4 * xp)
@@ -271,24 +274,23 @@
         share(h, p, 2).start()
 
     def take(h, way):
-        for p in range(2):
+        for p in range(PARTS):
             arrived(h, p, way)
         first(source(h, way))
 
-    own(0, 0)
-    own(0, 1)
-    first(g)
-    forward(0, 0)
-    take(0, 0)
-    own(1, 0)
-    forward(0, 1)
-    first(source(0, 1))
-    own(1, 1)
+    for t in range(2 * PARTS):
+        own(t // PARTS, t % PARTS)
+        if t > 0:
+            forward((t - 1) // PARTS, (t - 1) % PARTS)
+        if t == PARTS + 1:
+            first(g)
+            take(0, 0)
+        if t == PARTS + 2:
+            first(source(0, 1))
+            take(0, 2)
     first(4 + g)
-    forward(1, 0)
-    take(0, 2)
     take(1, 0)
-    forward(1, 1)
+    forward(1, PARTS - 1)
     first(source(1, 1))
     take(1, 2)
 
@@ -340,12 +342,12 @@
         value = second(4 * h + 2 * (1 - xp) + core)
         sib_copies[h, 0].wait_recv()
         pair[2 + h] = (value + from_sib[2 * h].astype(F32)).astype(BF16)
-        for p in range(2):
+        for p in range(PARTS):
             nbr_copies[h, p] = pltpu.make_async_remote_copy(
                 src_ref=pair.at[2 + h, part(p)],
                 dst_ref=from_nbr.at[h, part(p)],
-                send_sem=red_s.at[4 + 2 * h + p],
-                recv_sem=red_r.at[4 + 2 * h + p],
+                send_sem=red_s.at[4 + PARTS * h + p],
+                recv_sem=red_r.at[4 + PARTS * h + p],
                 device_id=nbr,
                 device_id_type=MESH,
             )
@@ -357,7 +359,7 @@
         sib_copies[h, 1].wait_recv()
         mine[h] = value + from_sib[2 * h + 1].astype(F32)
     for h in range(2):
-        for p in range(2):
+        for p in range(PARTS):
             nbr_copies[h, p].wait_recv()
             pair[h, part(p)] = (
                 mine[h, part(p)] + from_nbr[h, part(p)].astype(F32)
@@ -374,17 +376,17 @@
                 ).start()
                 return carry
 
-            lax.fori_loop(max(1, p * (n // 2)), (p + 1) * (n // 2), go_back, 0)
+            lax.fori_loop(max(1, p * (n // PARTS)), (p + 1) * (n // PARTS), go_back, 0)
         back[h, 0] = pair[h, 0]
 
-    half_rows = rows16 // 2
+    part_rows = rows16 // PARTS
     for h in range(2):
         sums = None
-        for p in range(2):
+        for p in range(PARTS):
             bulk_wait(back.at[h, landed(p)], epr2.at[h, p])
             more = dot(
-                sel[:, p * half_rows : (p + 1) * half_rows],
-                back[h, part(p)].reshape(half_rows, lanes),
+                sel[:, p * part_rows : (p + 1) * part_rows],
+                back[h, part(p)].reshape(part_rows, lanes),
             )
             sums = more if p == 0 else sums + more
         for q in range(2):
@@ -414,14 +416,13 @@
     total = fin[u].astype(F32)
     for v in range(1, 8):
         total = total + fin_in[v].astype(F32)
-    mixed[...] = total[:tok_rows].astype(BF16)
-    d_tok[...] = total[tok_rows:].astype(BF16)
+    sums_out[...] = total.astype(BF16)
 
     bulk_wait(fin_in.at[pl.ds(1, 7)], fin_s)
     for h in range(2):
         bulk_wait(send.at[h, pl.ds(1, n - 1)], eps.at[h])
         bulk_wait(pair.at[h, pl.ds(1, n - 1)], eps2.at[h])
-        for p in range(2):
+        for p in range(PARTS):
             for way in range(3):
                 share(h, p, way).wait_send()
             nbr_copies[h, p].wait_send()
@@ -446,17 +447,17 @@
     lanes = 2 * BLK
     vmem = pl.BlockSpec(memory_space=pltpu.VMEM)
     hbm = pl.BlockSpec(memory_space=pl.ANY)
-    out = jax.ShapeDtypeStruct((tok_rows, BLK), BF16)
+    out = jax.ShapeDtypeStruct((2 * tok_rows, BLK), BF16)
     dma = pltpu.SemaphoreType.DMA
 
     def body(*refs):
         kernel(n, *refs)
 
-    return pl.pallas_call(
+    sums = pl.pallas_call(
         body,
-        out_shape=(out, out),
+        out_shape=out,
         in_specs=[hbm] * 10,
-        out_specs=(vmem, vmem),
+        out_specs=vmem,
         scratch_shapes=[
             pltpu.VMEM((tok_rows, width), BF16),
             pltpu.VMEM((tok_rows, width), BF16),
@@ -487,13 +488,13 @@
             pltpu.VMEM((8, 2 * tok_rows, BLK), BF16),
             dma((10,)),
             dma((2,)),
-            dma((2, 2)),
-            dma((2, 2, 3)),
-            dma((2, 2, 3)),
-            dma((8,)),
-            dma((8,)),
+            dma((2, PARTS)),
+            dma((2, PARTS, 3)),
+            dma((2, PARTS, 3)),
+            dma((4 + 2 * PARTS,)),
+            dma((4 + 2 * PARTS,)),
             dma((2,)),
-            dma((2, 2)),
+            dma((2, PARTS)),
             dma,
             dma,
         ],
@@ -517,6 +518,7 @@
         up_codes,
         down_codes,
     )
+    return sums[:tok_rows], sums[tok_rows:]
 
 
 def solution(mesh):

time: 82 us -> 81.2 us (level)
    unnamed x4 -> x0, local copies, waits for them, and re-layouts: 1.92 us -> none
    slice x0 -> x1, local copies, waits for them, and re-layouts: none -> 1.33 us  [per_device(): return (sums[:tok_rows], sums[tok_rows:])]
where the time goes in v3:
time: 81.2 us; the launch traced here: 80.3 us
  Pallas kernels  78.3 us (96%)
  local copies, waits for them, and re-layouts  1.33 us (2%)
    pallas_call x1, Pallas kernels, per_device(): pl.pallas_call(body, out_shape=out, in_specs=[hbm] * 10, out_specs=vmem,...  78.3 us

profile of v3, /device:TPU:14, one launch (start us, length us, event | category | flops | bytes accessed | tf_op | source)
XLA Modules:
  0.0 80.3 jit_solution(12640190510298782871)
XLA Ops:
  0.6 78.3 %shard_map.113 = bf16[96,128]{1,0:T(8,128)(2,1)} custom-call(bf16[48,4096]{1,0:T(8,128)(2,1)} %refs_0_.1, bf16[48,4096]{1,0:T(8,128)(2,1)} %refs_1_.1, s32[8,48]{1,0:T(8,128)} %bitcast.4, f32[8,48]{1,0:T(8,128)} %bitcast.5, f32[1,32]{1,0:T(1,128)} %bitcast.6, f32[1,32]{1,0:T(1,128)} %bitcast.7, f32[1,32]{1,0:T(1,128)} %refs_6_.1, bf16[4096,128]{1,0:T(8,128)(2,1)} %refs_7_.1, ...), custom_call_target="tpu_custom_call" | custom-call | flops 2415919104 | bytes 3145728 | tf_op jit(solution)/shard_map/pallas_call | solution.py:456
  79.0 1.3 %fusion = (bf16[48,128]{1,0:T(8,128)(2,1)}, bf16[48,128]{1,0:T(8,128)(2,1)}) fusion(bf16[96,128]{1,0:T(8,128)(2,1)} %shard_map.113), kind=kLoop, calls=%fused_computation | loop fusion | bytes 49152 | tf_op jit(solution)/shard_map/slice | solution.py:521
